TPU v7x, 32 devices: a whole 2x2x4 slice. The times are simulated.
32 devices in a mesh: ctx: 8 (over z, y), tp: 4 (over x, core).
Axes of the slice: x: 2, y: 2, z: 4, core: 2. Of those that a mesh axis runs over, the one named last changes fastest.
Arguments:
- query_proj: bfloat16 [1024, 4096], P('ctx', 'tp'), may hold values from -6 to 6
- key_proj: bfloat16 [1024, 4096], P('ctx', 'tp'), may hold values from -6 to 6
- value_proj: bfloat16 [1024, 4096], P('ctx', 'tp'), may hold values from -6 to 6
- filters: float32 [256, 128], P('tp'), may hold values from -0.5 to 0.5
- skip_gain: float32 [4096], P('tp'), may hold values from -1 to 1
- out_grad: bfloat16 [1024, 4096], P('ctx', 'tp'), may hold values from -6 to 6
- w_out: bfloat16 [4096, 4096], P('tp'), may hold values from -0.09375 to 0.09375
Outputs:
- query_grad: bfloat16 [1024, 4096], P('ctx', 'tp')
- key_grad: bfloat16 [1024, 4096], P('ctx', 'tp')
- value_grad: bfloat16 [1024, 4096], P('ctx', 'tp')
- filter_grad: float32 [256, 128], P('tp')
- skip_grad: float32 [4096], P('tp')
All inputs are finite; a program needn't handle non-finite values.
Results may differ from a plain program's by a relative error of at most 0.0075.
Values may be sent and summed in bfloat16 or wider, within the bound.
A program may use at most 128 MiB of HBM per device.

v0:
```python
import jax
import jax.numpy as jnp
from jax import lax
from jax.sharding import PartitionSpec as P


def passed_along(block, axis, distance):
    devices = range(lax.axis_size(axis))
    route = [(i - distance, i) for i in devices if i - distance in devices]
    return lax.ppermute(block, axis, route)


def blocks_of(extended, width):
    count = (extended.shape[0] - width) // width
    channels = extended.shape[1]
    first = extended[:-width].reshape(count, width, channels)
    second = extended[width:].reshape(count, width, channels)
    return jnp.concatenate([first, second], axis=1)


def tap_table(filters, causal):
    width = filters.shape[1]
    rows = jnp.arange(width)[:, None]
    cols = jnp.arange(2 * width)[None, :]
    lag = rows + width - cols if causal else cols - rows
    valid = (lag >= 0) & (lag < width)
    index = jnp.clip(lag, 0, width - 1)
    table = filters[:, index]
    return jnp.where(valid[None], table, jnp.float32(0.0))


def convolve(extended, filters, skip_gain, causal):
    width = filters.shape[1]
    groups = filters.shape[0]
    channels = extended.shape[1]
    window = blocks_of(extended, width)
    count = window.shape[0]
    window = window.reshape(count, 2 * width, groups, channels // groups).astype(jnp.float32)
    mixed = jnp.einsum(
        "gij,bjgc->bigc", tap_table(filters, causal), window, precision=lax.Precision.HIGHEST
    )
    mixed = mixed.reshape(count * width, channels)
    current = extended[width:] if causal else extended[:-width]
    return mixed + skip_gain[None, :] * current.astype(jnp.float32)


def diagonal_lags(pairs, width):
    leading = pairs.shape[:-2]
    flat = pairs.reshape(leading + (width * 2 * width,))
    padded = jnp.concatenate([flat, jnp.zeros(leading + (width,), jnp.float32)], axis=-1)
    skewed = padded.reshape(leading + (width, 2 * width + 1)).sum(axis=-2)
    return skewed[..., width:0:-1]


def on_device(query_proj, key_proj, value_proj, filters, skip_gain, out_grad, w_out):
    width = filters.shape[1]
    groups = filters.shape[0]
    tok_rows = query_proj.shape[0]
    channels = query_proj.shape[1]
    span = channels // groups
    rim_rows = width - 1
    count = tok_rows // width
    query_f = query_proj.astype(jnp.float32)
    key_f = key_proj.astype(jnp.float32)
    value_f = value_proj.astype(jnp.float32)
    products = (key_f * value_f).astype(jnp.bfloat16)
    product_f = products.astype(jnp.float32)
    mixer_grad = lax.dot_general(
        lax.all_gather(out_grad, "tp", axis=1, tiled=True),
        w_out,
        (((1,), (1,)), ((), ())),
        preferred_element_type=jnp.float32,
    )
    earlier = passed_along(products[tok_rows - rim_rows :], "ctx", 1)
    single = jnp.zeros((1, channels), jnp.bfloat16)
    prod_ext = jnp.concatenate([single, earlier, products], axis=0)
    filtered = convolve(prod_ext, filters, skip_gain, True)
    query_grad = (mixer_grad * filtered).astype(jnp.bfloat16)
    filtered_grad = (mixer_grad * query_f).astype(jnp.bfloat16)
    grad_f = filtered_grad.astype(jnp.float32)
    later = passed_along(filtered_grad[:rim_rows], "ctx", -1)
    grad_ext = jnp.concatenate([filtered_grad, later, single], axis=0)
    product_grad = convolve(grad_ext, filters, skip_gain, False)
    key_grad = (product_grad * value_f).astype(jnp.bfloat16)
    value_grad = (product_grad * key_f).astype(jnp.bfloat16)
    window = blocks_of(prod_ext, width)
    grad_blocks = filtered_grad.reshape(count, width, channels)
    skip_part = jnp.sum(grad_f * product_f, axis=0)
    pairs = jnp.einsum(
        "bigc,bjgc->gij",
        grad_blocks.reshape(count, width, groups, span),
        window.reshape(count, 2 * width, groups, span),
        preferred_element_type=jnp.float32,
    )
    grouped = diagonal_lags(pairs, width)
    filter_grad, skip_grad = lax.psum((grouped, skip_part), "ctx")
    return (query_grad, key_grad, value_grad, filter_grad, skip_grad)


def solution(mesh):
    return jax.shard_map(
        on_device,
        mesh=mesh,
        in_specs=(
            P("ctx", "tp"),
            P("ctx", "tp"),
            P("ctx", "tp"),
            P("tp", None),
            P("tp"),
            P("ctx", "tp"),
            P("tp", None),
        ),
        out_specs=(P("ctx", "tp"), P("ctx", "tp"), P("ctx", "tp"), P("tp", None), P("tp")),
        check_vma=False,
    )
```

profile of v0, /device:TPU:0, one launch (start us, length us, event | category | flops | bytes accessed | tf_op | source)
XLA Modules:
  0.0 376.2 jit_solution(13880040861033989793)
XLA Ops:
  7.2 0.7 all-gather.2.cloned.1.call-update
  8.3 20.7 %all-gather.2.cloned.1.call-done = bf16[128,4096]{1,0:T(8,128)(2,1)} async-done(((bf16[128,1024]{1,0:T(8,128)(2,1)}), bf16[128,4096]{1,0:T(8,128)(2,1)}) %all-gather.2.cloned.1.call-update) | async-done | bytes 1048592 | tf_op jit(solution)/shard_map/all_gather | solution.py:69
  29.0 6.7 %fusion.17 = (f32[1024]{0:T(1024)S(1)}, bf16[128,1024]{1,0:T(8,128)(2,1)S(1)}, bf16[128,1024]{1,0:T(8,128)(2,1)S(1)}, f32[128,1024]{1,0:T(8,128)S(1)}) fusion(bf16[128,1024]{1,0:T(8,128)(2,1)} %param.7, bf16[128,1024]{1,0:T(8,128)(2,1)} %param.9, bf16[128,1024]{1,0:T(8,128)(2,1)} %param.8, bf16[128,4096]{1,0:T(8,128)(2,1)} %all-gather.2.cloned.1.call-done, ...), kind=kOutput, calls=%fused_computation.25 | convolution fusion | flops 1075182592 | bytes 11276288 | tf_op jit(solution)/shard_map/dot_general | solution.py:68
  35.8 1.3 collective-permute-start.1
  37.2 108.4 %gather_fusion.1 = f32[32768,64]{1,0:T(8,128)} fusion(f32[64,128]{0,1:T(8,128)S(1)} %copy.25, s32[32768]{0:T(1024)S(1)} %broadcast_clamp_fusion), kind=kCustom, calls=%fused_computation.1 | custom fusion | bytes 16908288 | tf_op jit(solution)/shard_map/gather | solution.py:28
  145.6 13.6 %copy.31 = f32[128,256,64]{1,0,2:T(8,128)} copy(f32[128,256,64]{2,1,0:T(8,128)} %bitcast.45) | data formatting | bytes 16777216 | tf_op jit(solution)/shard_map/gather | solution.py:28
  159.2 108.3 %gather_fusion = f32[32768,64]{1,0:T(8,128)} fusion(f32[64,128]{0,1:T(8,128)S(1)} %copy.25, s32[32768]{0:T(1024)S(1)} %broadcast_clamp_fusion.1), kind=kCustom, calls=%fused_computation | custom fusion | bytes 16908288 | tf_op jit(solution)/shard_map/gather | solution.py:28
  267.5 13.6 %copy.26 = f32[128,256,64]{1,0,2:T(8,128)} copy(f32[128,256,64]{2,1,0:T(8,128)} %bitcast.44) | data formatting | bytes 16777216 | tf_op jit(solution)/shard_map/gather | solution.py:28
  281.2 0.2 copy.28
  281.4 0.2 copy.24
  281.6 4.7 %collective-permute-start = (bf16[127,1024]{1,0:T(8,128)(2,1)S(1)}, bf16[127,1024]{1,0:T(8,128)(2,1)S(1)}, u32[]{:S(2)}, u32[]{:S(2)}) collective-permute-start(bf16[127,1024]{1,0:T(8,128)(2,1)S(1)} %slice.19), channel_id=1, source_target_pairs={{0,4},{4,8},{8,12},{12,16},{16,20},{20,24},{24,28},{1,5},{5,9},{9,... | collective-permute-start | bytes 780296 | tf_op jit(solution)/shard_map/ppermute | solution.py:10
  286.4 0.2 copy.35
  286.6 6.5 %fusion = f32[64,16,128]{2,1,0:T(8,128)S(1)} fusion(f32[128,256,64]{1,0,2:T(8,128)} %copy.31, pred[128,256]{1,0:T(8,128)(4,1)S(1)} %fusion.28, bf16[1,128,64,16]{1,3,2,0:T(8,128)(2,1)S(1)} %bitcast.57, bf16[1,128,64,16]{1,3,2,0:T(8,128)(2,1)S(1)} %bitcast.50), kind=kOutput, calls=%fused_computation.2 | convolution fusion | flops 405798912 | bytes 9469952 | tf_op jit(solution)/shard_map/gij,bjgc->bigc/dot_general | solution.py:39
  293.2 0.2 copy.32
  293.4 0.2 copy.34
  293.7 6.5 %fusion.2 = f32[64,16,128]{2,1,0:T(8,128)S(1)} fusion(f32[128,256,64]{1,0,2:T(8,128)} %copy.26, pred[128,256]{1,0:T(8,128)(4,1)S(1)} %fusion.27, bf16[1,128,64,16]{1,3,2,0:T(8,128)(2,1)S(1)} %bitcast.52, bf16[1,128,64,16]{1,3,2,0:T(8,128)(2,1)S(1)} %bitcast.48), kind=kOutput, calls=%fused_computation.4 | convolution fusion | flops 405798912 | bytes 9469952 | tf_op jit(solution)/shard_map/gij,bjgc->bigc/dot_general | solution.py:39
  300.3 0.2 copy.27
  300.5 1.3 fusion.20
  301.8 4.7 %copy.38 = f32[8,8,128,256]{3,1,2,0:T(8,128)S(1)} copy(f32[8,8,128,256]{3,2,1,0:T(8,128)S(1)} %bitcast.47) | data formatting | bytes 16777216
  306.5 3.8 concatenate.35
  310.3 14.2 %reshape.171 = f32[64,128,257]{2,1,0:T(8,128)} reshape(f32[64,32896]{1,0:T(8,128)} %concatenate.35) | data formatting | bytes 16842752 | tf_op jit(solution)/shard_map/reshape | solution.py:51
  324.4 6.1 %reduce_sum.18 = f32[64,257]{1,0:T(8,128)S(1)} reduce(f32[64,128,257]{2,1,0:T(8,128)} %reshape.171, f32[]{:T(128)} %constant.1.clone.1), dimensions={1}, to_apply=%region_0.1 | reduce | flops 2088896 | bytes 8487172 | tf_op jit(solution)/shard_map/reduce_sum | solution.py:51
  330.7 37.5 %all-reduce.3 = (f32[64,128]{1,0:T(8,128)}, f32[1024]{0:T(1024)}) all-reduce(f32[64,128]{1,0:T(8,128)S(1)} %rev.3, f32[1024]{0:T(1024)S(1)} %get-tuple-element.7), channel_id=1, replica_groups=mesh['ctx'=8,'tp'=4] {'ctx'}, use_global_device_ids=true, to_apply=%region_1.2 | all-reduce | flops 9216 | bytes 73728 | tf_op jit(solution)/shard_map/psum | solution.py:96
  368.3 1.1 fusion.10
  (26 shorter events, 1.0 us)
Async XLA Ops:
  7.2 29.9 %copy-start.2 = (f32[64,128]{1,0:T(8,128)S(1)}, f32[64,128]{1,0:T(8,128)}, u32[]{:S(2)}) copy-start(f32[64,128]{1,0:T(8,128)} %param.10) | copy-start | bytes 98308
  7.2 21.9 %all-gather.2.cloned.1.call-start = ((), (), s32[]{:S(2)}) async-start(), calls=%async_computation | async-start | bytes 1310720 | tf_op jit(solution)/shard_map/all_gather | solution.py:69
  35.8 250.6 %collective-permute-start.1 = (bf16[127,1024]{1,0:T(8,128)(2,1)S(1)}, bf16[127,1024]{1,0:T(8,128)(2,1)S(1)}, u32[]{:S(2)}, u32[]{:S(2)}) collective-permute-start(bf16[127,1024]{1,0:T(8,128)(2,1)S(1)} %bitcast.54), channel_id=1, source_target_pairs={{4,0},{8,4},{12,8},{16,12},{20,16},{24,20},{28,24},{5,1},{9,5},{13... | collective-permute-start | bytes 780296 | tf_op jit(solution)/shard_map/ppermute | solution.py:10
  281.6 11.8 %collective-permute-start = (bf16[127,1024]{1,0:T(8,128)(2,1)S(1)}, bf16[127,1024]{1,0:T(8,128)(2,1)S(1)}, u32[]{:S(2)}, u32[]{:S(2)}) collective-permute-start(bf16[127,1024]{1,0:T(8,128)(2,1)S(1)} %slice.19), channel_id=1, source_target_pairs={{0,4},{4,8},{8,12},{12,16},{16,20},{20,24},{24,28},{1,5},{5,9},{9,... | collective-permute-start | bytes 780296 | tf_op jit(solution)/shard_map/ppermute | solution.py:10
  324.4 43.8 %copy-start = (bf16[128,1024]{1,0:T(8,128)(2,1)S(1)}, bf16[128,1024]{1,0:T(8,128)(2,1)}, u32[]{:S(2)}) copy-start(bf16[128,1024]{1,0:T(8,128)(2,1)} %param.8) | copy-start | bytes 786436
  324.4 43.8 %copy-start.1 = (bf16[128,1024]{1,0:T(8,128)(2,1)S(1)}, bf16[128,1024]{1,0:T(8,128)(2,1)}, u32[]{:S(2)}) copy-start(bf16[128,1024]{1,0:T(8,128)(2,1)} %param.9) | copy-start | bytes 786436
  324.4 43.8 %copy-start.3 = (f32[1024]{0:T(1024)S(1)}, f32[1024]{0:T(1024)}, u32[]{:S(2)}) copy-start(f32[1024]{0:T(1024)} %param.11) | copy-start | bytes 12292
Sparse Core Ops, SparseCore 0:
  9.6 19.4 all-gather.1
where the time goes:
time: 377 us; the launch traced here: 376 us
  local copies, waits for them, and re-layouts  268 us (71%)
  blocking collectives  37.5 us (10%)
  waiting for transfers between devices  21.4 us (6%)
  matrix products  21.1 us (6%)
  between operations  14.2 us (4%)
  other arithmetic  7.52 us (2%)
  starting transfers between devices  6.07 us (2%)
    gather x4, local copies, waits for them, and re-layouts, tap_table(): table = filters[:, index]  244 us
    psum x1, blocking collectives, on_device(): filter_grad, skip_grad = lax.psum((grouped, skip_part), 'ctx')  37.5 us
    all_gather x1, waiting for transfers between devices, on_device(): lax.all_gather(out_grad, 'tp', axis=1, tiled=True)  20.7 us
    reshape x1, local copies, waits for them, and re-layouts, diagonal_lags(): skewed = padded.reshape(leading + (width, 2 * width + 1)).sum(axis=-2)  14.2 us
    dot_general x2, matrix products, convolve(): jnp.einsum('gij,bjgc->bigc', tap_table(filters, causal), window, precisio...  13.1 us
  transfers between devices with their start and end apart: 3, of which 1 were waited for; matrix products, arithmetic and copies ran while one was open for 67% of the time, Pallas kernels for 0%

commit v1 on v0

--- a/solution.py
+++ b/solution.py
@@ -2,6 +2,29 @@
 import jax.numpy as jnp
 from jax import lax
 from jax.sharding import PartitionSpec as P
+
+
+def laid_out(blocks, dim):
+    shape = list(blocks.shape[1:])
+    shape[dim] *= blocks.shape[0]
+    return jnp.moveaxis(blocks, 0, dim).reshape(shape)
+
+
+def grow_blocks(value, axis):
+    size, index = (lax.axis_size(axis), lax.axis_index(axis))
+    pieces, bit = (value[None], 1)
+    while bit < size:
+        received = lax.ppermute(pieces, axis, [(i, i ^ bit) for i in range(size)])
+        low = index & bit == 0
+        pieces = jnp.concatenate(
+            [jnp.where(low, pieces, received), jnp.where(low, received, pieces)]
+        )
+        bit *= 2
+    return pieces
+
+
+def gather_by_bits(x, axis, dim):
+    return laid_out(grow_blocks(x, axis), dim)
 
 
 def passed_along(block, axis, distance):
@@ -66,7 +89,7 @@
     products = (key_f * value_f).astype(jnp.bfloat16)
     product_f = products.astype(jnp.float32)
     mixer_grad = lax.dot_general(
-        lax.all_gather(out_grad, "tp", axis=1, tiled=True),
+        gather_by_bits(out_grad, "tp", 1),
         w_out,
         (((1,), (1,)), ((), ())),
         preferred_element_type=jnp.float32,

time: 377 us -> 360 us (0.955)
  between operations: 14.2 us -> 0.88 us
  waiting for transfers between devices: 21.4 us -> 13 us
    all_gather x1 -> x0, waiting for transfers between devices: 20.7 us -> none  [on_device(): lax.all_gather(out_grad, 'tp', axis=1, tiled=True)]
    ppermute x0 -> x2, waiting for transfers between devices: none -> 13 us  [grow_blocks(): received = lax.ppermute(pieces, axis, [(i, i ^ bit) for i in range(size)])]
  transfers between devices with their start and end apart: 3 -> 4, of which waited for: 1 -> 2; matrix products, arithmetic and copies ran while one was open for 67% -> 70% of each run, Pallas kernels for 0% -> 0%
where the time goes in v1:
time: 360 us
  local copies, waits for them, and re-layouts  271 us (75%)
  blocking collectives  37.1 us (10%)
  matrix products  20.8 us (6%)
  waiting for transfers between devices  13 us (4%)
  starting transfers between devices  9.48 us (3%)
  other arithmetic  7.78 us (2%)
    gather x4, local copies, waits for them, and re-layouts, tap_table(): table = filters[:, index]  245 us
    psum x1, blocking collectives, on_device(): filter_grad, skip_grad = lax.psum((grouped, skip_part), 'ctx')  37.1 us
    reshape x1, local copies, waits for them, and re-layouts, diagonal_lags(): skewed = padded.reshape(leading + (width, 2 * width + 1)).sum(axis=-2)  14.2 us
    dot_general x2, matrix products, convolve(): jnp.einsum('gij,bjgc->bigc', tap_table(filters, causal), window, precisio...  13.1 us
    ppermute x2, waiting for transfers between devices, grow_blocks(): received = lax.ppermute(pieces, axis, [(i, i ^ bit) for i in range(size)])  13 us
  transfers between devices with their start and end apart: 4, of which 2 were waited for; matrix products, arithmetic and copies ran while one was open for 70% of the time, Pallas kernels for 0%

profile of v1, /device:TPU:0, one launch (start us, length us, event | category | flops | bytes accessed | tf_op | source)
XLA Modules:
  0.0 359.8 jit_solution(4110098657804011617)
XLA Ops:
  0.6 1.1 copy.23
  1.8 0.5 collective-permute-start
  2.6 0.8 collective-permute-done
  3.5 2.9 collective-permute-start.1
  6.5 12.2 %collective-permute-done.1 = bf16[2,128,1024]{1,2,0:T(8,128)(2,1)S(1)} collective-permute-done((bf16[2,128,1024]{1,2,0:T(8,128)(2,1)S(1)}, bf16[2,128,1024]{1,2,0:T(8,128)(2,1)S(1)}, u32[]{:S(2)}, u32[]{:S(2)}) %collective-permute-start.1) | collective-permute-done | bytes 524320 | tf_op jit(solution)/shard_map/ppermute | solution.py:17
  18.9 6.5 %fusion.17 = (f32[1024]{0:T(1024)S(1)}, bf16[128,1024]{1,0:T(8,128)(2,1)S(1)}, bf16[128,1024]{1,0:T(8,128)(2,1)S(1)}, f32[128,1024]{1,0:T(8,128)S(1)}) fusion(bf16[128,1024]{1,0:T(8,128)(2,1)} %param.7, bf16[128,1024]{1,0:T(8,128)(2,1)} %param.9, bf16[128,1024]{1,0:T(8,128)(2,1)} %param.8, bf16[128,4096]{0,1:T(8,128)(2,1)S(1)} %bitcast.54, ...), kind=kOutput, calls=%fused_computation.26 | convolution fusion | flops 1075182592 | bytes 11276288 | tf_op jit(solution)/shard_map/dot_general | solution.py:91
  25.4 1.3 collective-permute-start.3
  26.8 109.0 %gather_fusion.1 = f32[32768,64]{1,0:T(8,128)} fusion(f32[64,128]{0,1:T(8,128)S(1)} %copy.26, s32[32768]{0:T(1024)S(1)} %broadcast_clamp_fusion), kind=kCustom, calls=%fused_computation.1 | custom fusion | bytes 16908288 | tf_op jit(solution)/shard_map/gather | solution.py:51
  135.8 13.6 %copy.32 = f32[128,256,64]{1,0,2:T(8,128)} copy(f32[128,256,64]{2,1,0:T(8,128)} %bitcast.51) | data formatting | bytes 16777216 | tf_op jit(solution)/shard_map/gather | solution.py:51
  149.4 109.0 %gather_fusion = f32[32768,64]{1,0:T(8,128)} fusion(f32[64,128]{0,1:T(8,128)S(1)} %copy.26, s32[32768]{0:T(1024)S(1)} %broadcast_clamp_fusion.1), kind=kCustom, calls=%fused_computation | custom fusion | bytes 16908288 | tf_op jit(solution)/shard_map/gather | solution.py:51
  258.4 13.6 %copy.27 = f32[128,256,64]{1,0,2:T(8,128)} copy(f32[128,256,64]{2,1,0:T(8,128)} %bitcast.50) | data formatting | bytes 16777216 | tf_op jit(solution)/shard_map/gather | solution.py:51
  272.5 4.7 %collective-permute-start.2 = (bf16[127,1024]{1,0:T(8,128)(2,1)S(1)}, bf16[127,1024]{1,0:T(8,128)(2,1)S(1)}, u32[]{:S(2)}, u32[]{:S(2)}) collective-permute-start(bf16[127,1024]{1,0:T(8,128)(2,1)S(1)} %slice.19), channel_id=1, source_target_pairs={{0,4},{4,8},{8,12},{12,16},{16,20},{20,24},{24,28},{1,5},{5,9},{9,... | collective-permute-start | bytes 780296 | tf_op jit(solution)/shard_map/ppermute | solution.py:33
  277.3 0.2 copy.36
  277.5 6.5 %fusion = f32[64,16,128]{2,1,0:T(8,128)S(1)} fusion(f32[128,256,64]{1,0,2:T(8,128)} %copy.32, pred[128,256]{1,0:T(8,128)(4,1)S(1)} %fusion.28, bf16[1,128,64,16]{1,3,2,0:T(8,128)(2,1)S(1)} %bitcast.64, bf16[1,128,64,16]{1,3,2,0:T(8,128)(2,1)S(1)} %bitcast.57), kind=kOutput, calls=%fused_computation.2 | convolution fusion | flops 405798912 | bytes 9469952 | tf_op jit(solution)/shard_map/gij,bjgc->bigc/dot_general | solution.py:62
  284.0 0.2 copy.33
  284.6 6.5 %fusion.2 = f32[64,16,128]{2,1,0:T(8,128)S(1)} fusion(f32[128,256,64]{1,0,2:T(8,128)} %copy.27, pred[128,256]{1,0:T(8,128)(4,1)S(1)} %fusion.27, bf16[1,128,64,16]{1,3,2,0:T(8,128)(2,1)S(1)} %bitcast.59, bf16[1,128,64,16]{1,3,2,0:T(8,128)(2,1)S(1)} %bitcast.55), kind=kOutput, calls=%fused_computation.4 | convolution fusion | flops 405798912 | bytes 9469952 | tf_op jit(solution)/shard_map/gij,bjgc->bigc/dot_general | solution.py:62
  291.1 0.2 copy.28
  291.3 1.3 fusion.20
  292.6 4.7 %copy.39 = f32[8,8,128,256]{3,1,2,0:T(8,128)S(1)} copy(f32[8,8,128,256]{3,2,1,0:T(8,128)S(1)} %bitcast.53) | data formatting | bytes 16777216
  297.4 3.7 %concatenate.43 = f32[64,32896]{1,0:T(8,128)} pad(f32[64,32768]{1,0:T(8,128)S(1)} %bitcast.52, f32[]{:T(128)} %constant.4.clone.1), padding=0_0x0_128 | pad | bytes 16809988 | tf_op jit(solution)/shard_map/concatenate | solution.py:73
  301.1 14.2 %reshape.175 = f32[64,128,257]{2,1,0:T(8,128)} reshape(f32[64,32896]{1,0:T(8,128)} %concatenate.43) | data formatting | bytes 16842752 | tf_op jit(solution)/shard_map/reshape | solution.py:74
  315.3 6.1 %reduce_sum.18 = f32[64,257]{1,0:T(8,128)S(1)} reduce(f32[64,128,257]{2,1,0:T(8,128)} %reshape.175, f32[]{:T(128)} %constant.4.clone.1), dimensions={1}, to_apply=%region_0.1 | reduce | flops 2088896 | bytes 8487172 | tf_op jit(solution)/shard_map/reduce_sum | solution.py:74
  321.6 37.1 %all-reduce.3 = (f32[64,128]{1,0:T(8,128)}, f32[1024]{0:T(1024)}) all-reduce(f32[64,128]{1,0:T(8,128)S(1)} %rev.3, f32[1024]{0:T(1024)S(1)} %get-tuple-element.7), channel_id=1, replica_groups=mesh['ctx'=8,'tp'=4] {'ctx'}, use_global_device_ids=true, to_apply=%region_1.2 | all-reduce | flops 9216 | bytes 73728 | tf_op jit(solution)/shard_map/psum | solution.py:119
  358.7 1.1 fusion.10
  (32 shorter events, 1.7 us)
Async XLA Ops:
  1.8 1.7 collective-permute-start
  3.5 23.2 %copy-start.2 = (f32[64,128]{1,0:T(8,128)S(1)}, f32[64,128]{1,0:T(8,128)}, u32[]{:S(2)}) copy-start(f32[64,128]{1,0:T(8,128)} %param.10) | copy-start | bytes 98308
  3.5 15.2 %collective-permute-start.1 = (bf16[2,128,1024]{1,2,0:T(8,128)(2,1)S(1)}, bf16[2,128,1024]{1,2,0:T(8,128)(2,1)S(1)}, u32[]{:S(2)}, u32[]{:S(2)}) collective-permute-start(bf16[2,128,1024]{1,2,0:T(8,128)(2,1)S(1)} %pad_maximum_fusion.1), channel_id=1, source_target_pairs={{0,2},{1,3},{2,0},{3,1},{4,6},{5,7},{6,4},{7,5},{8,10},{9,11},{10,... | collective-permute-start | bytes 1572872 | tf_op jit(solution)/shard_map/ppermute | solution.py:17
  25.4 251.9 %collective-permute-start.3 = (bf16[127,1024]{1,0:T(8,128)(2,1)S(1)}, bf16[127,1024]{1,0:T(8,128)(2,1)S(1)}, u32[]{:S(2)}, u32[]{:S(2)}) collective-permute-start(bf16[127,1024]{1,0:T(8,128)(2,1)S(1)} %bitcast.61), channel_id=1, source_target_pairs={{4,0},{8,4},{12,8},{16,12},{20,16},{24,20},{28,24},{5,1},{9,5},{13... | collective-permute-start | bytes 780296 | tf_op jit(solution)/shard_map/ppermute | solution.py:33
  272.5 11.8 %collective-permute-start.2 = (bf16[127,1024]{1,0:T(8,128)(2,1)S(1)}, bf16[127,1024]{1,0:T(8,128)(2,1)S(1)}, u32[]{:S(2)}, u32[]{:S(2)}) collective-permute-start(bf16[127,1024]{1,0:T(8,128)(2,1)S(1)} %slice.19), channel_id=1, source_target_pairs={{0,4},{4,8},{8,12},{12,16},{16,20},{20,24},{24,28},{1,5},{5,9},{9,... | collective-permute-start | bytes 780296 | tf_op jit(solution)/shard_map/ppermute | solution.py:33
  315.3 43.4 %copy-start = (bf16[128,1024]{1,0:T(8,128)(2,1)S(1)}, bf16[128,1024]{1,0:T(8,128)(2,1)}, u32[]{:S(2)}) copy-start(bf16[128,1024]{1,0:T(8,128)(2,1)} %param.8) | copy-start | bytes 786436
  315.3 43.4 %copy-start.1 = (bf16[128,1024]{1,0:T(8,128)(2,1)S(1)}, bf16[128,1024]{1,0:T(8,128)(2,1)}, u32[]{:S(2)}) copy-start(bf16[128,1024]{1,0:T(8,128)(2,1)} %param.9) | copy-start | bytes 786436
  315.3 43.4 %copy-start.3 = (f32[1024]{0:T(1024)S(1)}, f32[1024]{0:T(1024)}, u32[]{:S(2)}) copy-start(f32[1024]{0:T(1024)} %param.11) | copy-start | bytes 12292
